TPU v7x, 128 devices: a whole 4x4x4 slice. The times are simulated.
128 devices in a mesh: coord: 16 (over y_lo, x, core), ex: 8 (over y_hi, z).
Axes of the slice: x: 4, y: 4 (y_hi: 2, y_lo: 2; y = y_hi * 2 + y_lo), z: 4, core: 2. Of those that a mesh axis runs over, the one named last changes fastest.
Arguments:
- gradients: bfloat16 [4096, 65536], P('ex', 'coord'), may hold values from -6 to 6
- sign_flips: int32 [65536], P('coord'), may hold values from 0 to 1
- pick_offsets: int32 [4096], P('coord'), may hold values from 0 to 4095
- queries: bfloat16 [4096, 4096], P('ex', 'coord'), may hold values from -0.09375 to 0.09375
Outputs:
- scores: float32 [4096, 4096], P('ex', 'coord')
All inputs are finite; a program needn't handle non-finite values.
Results may differ from a plain program's by a relative error of at most 0.0029.
Values may be sent and summed in bfloat16 or wider, within the bound.
A program may use at most 128 MiB of HBM per device.

v0:
```python
import math

import jax
import jax.numpy as jnp
from jax import lax
from jax.sharding import PartitionSpec as P

INNER = 128
OUTER = 32


def partner_2(block, axis, apart):
    count = lax.axis_size(axis)
    route = []
    for low in range(count):
        high = low | 1 << apart
        if high != low and high < count:
            route += [(low, high), (high, low)]
    return lax.ppermute(block, axis, route)


def sylvester(matrix_order):
    counter = jnp.arange(matrix_order, dtype=jnp.int32)
    intersection = counter[:, None] & counter[None, :]
    parity = jnp.zeros_like(intersection)
    for bit_pos in range(matrix_order.bit_length() - 1):
        parity = parity + (intersection >> bit_pos & 1)
    return (1 - 2 * (parity % 2)).astype(jnp.float32)


def local_transform(gradients, sign_flips):
    row_count = gradients.shape[0]
    coord_width = gradients.shape[1]
    sign_values = (1 - 2 * sign_flips).astype(jnp.bfloat16)
    signed = (gradients * sign_values).reshape(row_count, OUTER, INNER)
    fast_table = sylvester(INNER).astype(jnp.bfloat16)
    slow_table = sylvester(OUTER)
    first_pass = jnp.einsum("rab,bc->rac", signed, fast_table, preferred_element_type=jnp.float32)
    second_pass = jnp.einsum("rab,ac->rcb", first_pass, slow_table, precision=lax.Precision.HIGHEST)
    return second_pass.reshape(row_count, coord_width)


def body(gradients, sign_flips, pick_offsets, queries):
    n_coord = lax.axis_size("coord")
    my_coord = lax.axis_index("coord")
    coord_width = gradients.shape[1]
    norm_scale = 1.0 / math.sqrt(coord_width * n_coord)
    section_bits = n_coord.bit_length() - 1
    local_image = local_transform(gradients, sign_flips)
    section_list = list(range(section_bits))
    current = local_image
    for bit_pos in section_list:
        partner = partner_2(current, "coord", bit_pos)
        upper_half = my_coord >> bit_pos & 1 == 1
        current = jnp.where(upper_half, partner - current, current + partner)
    picked = jnp.take(current, pick_offsets, axis=1) * norm_scale
    sketch = picked.astype(jnp.bfloat16)
    partial_value = jnp.dot(
        sketch,
        lax.all_gather(queries, "ex", axis=0, tiled=True).T,
        preferred_element_type=jnp.float32,
    )
    return lax.psum_scatter(partial_value, "coord", scatter_dimension=1, tiled=True)


def solution(mesh):
    in_specs = (P("ex", "coord"), P("coord"), P("coord"), P("ex", "coord"))
    out_specs = P("ex", "coord")
    return jax.shard_map(body, mesh=mesh, in_specs=in_specs, out_specs=out_specs, check_vma=False)
```

profile of v0, /device:TPU:1, one launch (start us, length us, event | category | flops | bytes accessed | tf_op | source)
XLA Modules:
  0.0 742.9 jit_solution(2468434617386743446)
XLA Ops:
  6.5 0.0 all-gather.2.cloned.1.call-start
  6.5 0.7 subtract_convert_fusion
  7.3 2.5 multiply_bitcast_fusion
  9.7 1.3 copy.9
  11.0 1.3 fusion.10
  12.3 9.4 %convolution_bitcast_fusion = f32[512,32,128]{2,1,0:T(8,128)} fusion(f32[512,32,128]{2,1,0:T(8,128)S(1)} %fusion.10), kind=kOutput, calls=%fused_computation.6 | convolution fusion | flops 805336064 | bytes 16777216 | tf_op jit(solution)/shard_map/rab,ac->rcb/dot_general | solution.py:39
  21.7 10.0 %copy.8 = f32[512,32,128]{0,2,1:T(8,128)} copy(f32[512,32,128]{2,1,0:T(8,128)} %convolution_bitcast_fusion) | data formatting | bytes 16777216 | tf_op jit(solution)/shard_map/reshape | solution.py:40
  31.7 1.4 collective-permute-start
  33.1 13.1 %collective-permute-done = f32[512,4096]{0,1:T(8,128)} collective-permute-done((f32[512,4096]{0,1:T(8,128)}, f32[512,4096]{0,1:T(8,128)}, u32[]{:S(2)}, u32[]{:S(2)}) %collective-permute-start) | collective-permute-done | bytes 8388640 | tf_op jit(solution)/shard_map/ppermute | solution.py:19
  46.2 11.1 %add_select_fusion.3 = f32[512,4096]{0,1:T(8,128)} fusion(f32[512,4096]{0,1:T(8,128)} %collective-permute-done, pred[]{:T(512)S(6)} %eq.19, f32[512,32,128]{0,2,1:T(8,128)} %copy.8), kind=kLoop, calls=%fused_computation.4 | loop fusion | flops 6291456 | bytes 25165824 | tf_op jit(solution)/shard_map/jit(_where)/select_n | solution.py:55
  57.4 1.3 collective-permute-start.1
  58.7 180.7 %collective-permute-done.1 = f32[512,4096]{0,1:T(8,128)} collective-permute-done((f32[512,4096]{0,1:T(8,128)}, f32[512,4096]{0,1:T(8,128)}, u32[]{:S(2)}, u32[]{:S(2)}) %collective-permute-start.1) | collective-permute-done | bytes 8388640 | tf_op jit(solution)/shard_map/ppermute | solution.py:19
  239.3 11.1 %add_select_fusion.2 = f32[512,4096]{0,1:T(8,128)} fusion(f32[512,4096]{0,1:T(8,128)} %add_select_fusion.3, f32[512,4096]{0,1:T(8,128)} %collective-permute-done.1, pred[]{:T(512)S(6)} %eq.18), kind=kLoop, calls=%fused_computation.3 | loop fusion | flops 6291456 | bytes 25165824 | tf_op jit(solution)/shard_map/jit(_where)/select_n | solution.py:55
  250.5 2.8 collective-permute-start.2
  253.3 0.0 copy-start
  253.3 179.7 %collective-permute-done.2 = f32[512,4096]{0,1:T(8,128)} collective-permute-done((f32[512,4096]{0,1:T(8,128)}, f32[512,4096]{0,1:T(8,128)}, u32[]{:S(2)}, u32[]{:S(2)}) %collective-permute-start.2) | collective-permute-done | bytes 8388640 | tf_op jit(solution)/shard_map/ppermute | solution.py:19
  433.0 11.1 %add_select_fusion.1 = f32[512,4096]{0,1:T(8,128)} fusion(f32[512,4096]{0,1:T(8,128)} %add_select_fusion.2, f32[512,4096]{0,1:T(8,128)} %collective-permute-done.2, pred[]{:T(512)S(6)} %eq.17), kind=kLoop, calls=%fused_computation.2 | loop fusion | flops 6291456 | bytes 25165824 | tf_op jit(solution)/shard_map/jit(_where)/select_n | solution.py:55
  444.2 1.4 collective-permute-start.3
  445.5 0.0 all-gather.2.cloned.1.call-update
  445.6 0.0 reduce-scatter.2.cloned.1.call-start
  445.6 0.0 copy-done
  445.7 192.7 %collective-permute-done.3 = f32[512,4096]{0,1:T(8,128)} collective-permute-done((f32[512,4096]{0,1:T(8,128)}, f32[512,4096]{0,1:T(8,128)}, u32[]{:S(2)}, u32[]{:S(2)}) %collective-permute-start.3) | collective-permute-done | bytes 8388640 | tf_op jit(solution)/shard_map/ppermute | solution.py:19
  638.3 11.1 %add_select_fusion = f32[512,4096]{0,1:T(8,128)} fusion(f32[512,4096]{0,1:T(8,128)} %add_select_fusion.1, f32[512,4096]{0,1:T(8,128)} %collective-permute-done.3, pred[]{:T(512)S(6)} %eq.16), kind=kLoop, calls=%fused_computation.1 | loop fusion | flops 6291456 | bytes 25165824 | tf_op jit(solution)/shard_map/jit(_where)/select_n | solution.py:55
  649.5 4.6 gather_fusion
  654.1 0.0 all-gather.2.cloned.1.call-done
  654.1 6.2 fusion
  660.3 0.0 reduce-scatter.2.cloned.1.call-update
  660.3 75.8 %reduce-scatter.2.cloned.1.call-done = f32[512,256]{1,0:T(8,128)} async-done(((f32[512,4096]{1,0:T(8,128)}), f32[512,256]{1,0:T(8,128)}) %reduce-scatter.2.cloned.1.call-update) | async-done | bytes 524304 | tf_op jit(solution)/shard_map/reduce_scatter | solution.py:63
  (3 shorter events, 0.0 us)
Async XLA Ops:
  6.5 647.5 %all-gather.2.cloned.1.call-start = ((), (), s32[]{:S(2)}) async-start(), calls=%async_computation.1 | async-start | bytes 2359296 | tf_op jit(solution)/shard_map/all_gather | solution.py:60
  31.7 14.5 %collective-permute-start = (f32[512,4096]{0,1:T(8,128)}, f32[512,4096]{0,1:T(8,128)}, u32[]{:S(2)}, u32[]{:S(2)}) collective-permute-start(f32[512,4096]{0,1:T(8,128)} %bitcast.16), channel_id=1, source_target_pairs={{0,8},{8,0},{16,24},{24,16},{32,40},{40,32},{48,56},{56,48},{64,72... | collective-permute-start | bytes 25165832 | tf_op jit(solution)/shard_map/ppermute | solution.py:19
  57.4 182.0 %collective-permute-start.1 = (f32[512,4096]{0,1:T(8,128)}, f32[512,4096]{0,1:T(8,128)}, u32[]{:S(2)}, u32[]{:S(2)}) collective-permute-start(f32[512,4096]{0,1:T(8,128)} %add_select_fusion.3), channel_id=1, source_target_pairs={{0,16},{16,0},{8,24},{24,8},{32,48},{48,32},{40,56},{56,40},{64,80... | collective-permute-start | bytes 25165832 | tf_op jit(solution)/shard_map/ppermute | solution.py:19
  250.5 182.6 %collective-permute-start.2 = (f32[512,4096]{0,1:T(8,128)}, f32[512,4096]{0,1:T(8,128)}, u32[]{:S(2)}, u32[]{:S(2)}) collective-permute-start(f32[512,4096]{0,1:T(8,128)} %add_select_fusion.2), channel_id=1, source_target_pairs={{0,32},{32,0},{8,40},{40,8},{16,48},{48,16},{24,56},{56,24},{64,96... | collective-permute-start | bytes 25165832 | tf_op jit(solution)/shard_map/ppermute | solution.py:19
  253.3 192.3 %copy-start = (s32[256]{0:T(256)S(1)}, s32[256]{0:T(256)}, u32[]{:S(2)}) copy-start(s32[256]{0:T(256)} %param.6) | copy-start | bytes 3076
  444.2 194.2 %collective-permute-start.3 = (f32[512,4096]{0,1:T(8,128)}, f32[512,4096]{0,1:T(8,128)}, u32[]{:S(2)}, u32[]{:S(2)}) collective-permute-start(f32[512,4096]{0,1:T(8,128)} %add_select_fusion.1), channel_id=1, source_target_pairs={{0,64},{64,0},{8,72},{72,8},{16,80},{80,16},{24,88},{88,24},{32,96... | collective-permute-start | bytes 25165832 | tf_op jit(solution)/shard_map/ppermute | solution.py:19
  445.6 290.5 %reduce-scatter.2.cloned.1.call-start = ((), (), s32[]{:S(2)}) async-start(), calls=%async_computation.2 | async-start | bytes 8912896 | tf_op jit(solution)/shard_map/reduce_scatter | solution.py:63
Sparse Core Ops, SparseCore 0:
  445.7 72.1 all-gather.1
  660.5 75.5 reduce-scatter.1
where the time goes:
time: 747 us; the launch traced here: 743 us
  waiting for transfers between devices  642 us (86%)
  other arithmetic  47.7 us (6%)
  matrix products  16.9 us (2%)
  local copies, waits for them, and re-layouts  15.8 us (2%)
  between operations  13.5 us (2%)
    ppermute x4, waiting for transfers between devices, partner_2(): return lax.ppermute(block, axis, route)  566 us
    reduce_scatter x1, waiting for transfers between devices, body(): lax.psum_scatter(partial_value, 'coord', scatter_dimension=1, tiled=True)  75.8 us
    select_n x4, other arithmetic, body(): current = jnp.where(upper_half, partner - current, current + partner)  44.5 us
  transfers between devices with their start and end apart: 6, of which 5 were waited for; matrix products, arithmetic and copies ran while one was open for 2% of the time, Pallas kernels for 0%

commit v1 on v0

v1 whole, which is shorter than its diff:
```python
import math

import jax
import jax.numpy as jnp
from jax import lax
from jax.sharding import PartitionSpec as P

INNER = 128


def parity_sign(left, right, bits):
    both = left & right
    parity = jnp.zeros_like(both)
    for bit in range(bits):
        parity = parity ^ (both >> bit & 1)
    return (1 - 2 * parity).astype(jnp.bfloat16)


def body(gradients, sign_flips, pick_offsets, queries):
    n_coord = lax.axis_size("coord")
    me = lax.axis_index("coord")
    rows, width = gradients.shape
    scale = 1.0 / math.sqrt(width * n_coord)
    signed = gradients * (1 - 2 * sign_flips).astype(jnp.bfloat16)
    offsets = lax.all_gather(pick_offsets, "coord", axis=0, tiled=True)
    segment = jnp.arange(offsets.shape[0], dtype=jnp.int32) // pick_offsets.shape[0]
    outer = width // INNER
    low = parity_sign(jnp.arange(INNER, dtype=jnp.int32)[:, None], (offsets % INNER)[None, :], 7)
    high = parity_sign(jnp.arange(outer, dtype=jnp.int32)[:, None], (offsets // INNER)[None, :], 5)
    far = parity_sign(segment, me, 4)
    table = (high * far[None, :])[:, None, :] * low[None, :, :]
    table = table.reshape(width, offsets.shape[0])
    partial = jnp.dot(signed, table, preferred_element_type=jnp.float32)
    picked = lax.psum_scatter(partial, "coord", scatter_dimension=1, tiled=True) * scale
    sketch = lax.all_gather(picked.astype(jnp.bfloat16), "coord", axis=1, tiled=True)
    mine = lax.all_gather(queries, "ex", axis=0, tiled=True)
    mine = lax.all_to_all(mine, "coord", split_axis=0, concat_axis=1, tiled=True)
    return jnp.dot(sketch, mine.T, preferred_element_type=jnp.float32)


def solution(mesh):
    in_specs = (P("ex", "coord"), P("coord"), P("coord"), P("ex", "coord"))
    return jax.shard_map(body, mesh=mesh, in_specs=in_specs, out_specs=P("ex", "coord"), check_vma=False)
```

time: 747 us -> 222 us (0.30)
  waiting for transfers between devices: 642 us -> 99 us
  blocking collectives: 0 us -> 61 us
  other arithmetic: 47.7 us -> 16.1 us
  local copies, waits for them, and re-layouts: 15.8 us -> 2.37 us
  matrix products: 16.9 us -> 27.9 us
    ppermute x4 -> x0, waiting for transfers between devices: 566 us -> none  [partner_2(): return lax.ppermute(block, axis, route)]
    select_n x5 -> x1, other arithmetic: 44.5 us -> 0.03 us  [body(): offsets // INNER]
    all_to_all x0 -> x1, blocking collectives: none -> 39.8 us  [body(): lax.all_to_all(mine, 'coord', split_axis=0, concat_axis=1, tiled=True)]
    all_gather x1 -> x2, waiting for transfers between devices: 0.02 us -> 28.7 us  [the longest x1 18.3 us: body(): lax.all_gather(picked.astype(jnp.bfloat16), 'coord', axis=1, tiled=True)]
    all_gather x0 -> x1, blocking collectives: none -> 21.2 us  [body(): offsets = lax.all_gather(pick_offsets, 'coord', axis=0, tiled=True)]
    mul x0 -> x2, other arithmetic: none -> 12 us  [body(): table = (high * far[None, :])[:, None, :] * low[None, :, :]]
    dot_general x3 -> x2, matrix products: 16.9 us -> 27.9 us  [the longest x1 23 us: body(): partial = jnp.dot(signed, table, preferred_element_type=jnp.float32)]
    reshape x1 -> x0, local copies, waits for them, and re-layouts: 10 us -> none  [local_transform(): return second_pass.reshape(row_count, coord_width)]
  transfers between devices with their start and end apart: 6 -> 3, of which waited for: 5 -> 3; matrix products, arithmetic and copies ran while one was open for 2% -> 2% of each run, Pallas kernels for 0% -> 0%
where the time goes in v1:
time: 222 us; the launch traced here: 221 us
  waiting for transfers between devices  99 us (45%)
  blocking collectives  61 us (27%)
  matrix products  27.9 us (13%)
  other arithmetic  16.1 us (7%)
  between operations  14.9 us (7%)
  local copies, waits for them, and re-layouts  2.37 us (1%)
    reduce_scatter x1, waiting for transfers between devices, body(): lax.psum_scatter(partial, 'coord', scatter_dimension=1, tiled=True) * scale  69.7 us
    all_to_all x1, blocking collectives, body(): lax.all_to_all(mine, 'coord', split_axis=0, concat_axis=1, tiled=True)  39.8 us
    dot_general x1, matrix products, body(): partial = jnp.dot(signed, table, preferred_element_type=jnp.float32)  23 us
    all_gather x1, blocking collectives, body(): offsets = lax.all_gather(pick_offsets, 'coord', axis=0, tiled=True)  21.2 us
    all_gather x1, waiting for transfers between devices, body(): lax.all_gather(picked.astype(jnp.bfloat16), 'coord', axis=1, tiled=True)  18.3 us
    mul x2, other arithmetic, body(): table = (high * far[None, :])[:, None, :] * low[None, :, :]  12 us
    all_gather x1, waiting for transfers between devices, body(): mine = lax.all_gather(queries, 'ex', axis=0, tiled=True)  10.5 us
    dot_general x1, matrix products, body(): return jnp.dot(sketch, mine.T, preferred_element_type=jnp.float32)  4.91 us
  transfers between devices with their start and end apart: 3, of which 3 were waited for; matrix products, arithmetic and copies ran while one was open for 2% of the time, Pallas kernels for 0%

profile of v1, /device:TPU:1, one launch (start us, length us, event | category | flops | bytes accessed | tf_op | source)
XLA Modules:
  0.0 221.3 jit_solution(6308974140431976200)
XLA Ops:
  7.4 0.0 reduce-scatter.2.cloned.1.call-start
  7.4 21.2 %all-gather = s32[16,1,256]{2,1,0:T(1,128)S(1)} all-gather(s32[1,1,256]{2,1,0:T(1,128)} %bitcast.14), channel_id=1, replica_groups=mesh['coord'=16,'ex'=8] {'coord'}, dimensions={0}, use_global_device_ids=true | all-gather | bytes 17408 | tf_op jit(solution)/shard_map/all_gather | solution.py:25
  28.6 1.6 subtract_convert_fusion
  30.2 0.7 subtract_convert_fusion.2
  31.0 0.3 fusion.3
  31.3 0.0 copy-start
  31.3 11.7 %broadcast_multiply_fusion = bf16[32,128,4096]{2,1,0:T(8,128)(2,1)} fusion(bf16[128,4096]{1,0:T(8,128)(2,1)S(1)} %subtract_convert_fusion, bf16[32,4096]{1,0:T(8,128)(2,1)S(1)} %fusion.3), kind=kLoop, calls=%fused_computation | loop fusion | flops 16777216 | bytes 34865152 | tf_op jit(solution)/shard_map/mul | solution.py:31
  43.0 0.0 copy-done
  43.0 23.0 %fusion = f32[512,4096]{1,0:T(8,128)} fusion(bf16[4096,4096]{1,0:T(8,128)(2,1)} %bitcast.9, bf16[512,4096]{1,0:T(8,128)(2,1)S(1)} %copy-done, bf16[4096]{0:T(1024)(128)(2,1)S(1)} %subtract_convert_fusion.2), kind=kOutput, calls=%fused_computation.1 | convolution fusion | flops 17181966336 | bytes 46145536 | tf_op jit(solution)/shard_map/dot_general | solution.py:33
  66.0 0.0 reduce-scatter.2.cloned.1.call-update
  66.0 0.0 all-gather.6.cloned.1.call-start
  66.0 0.5 all-gather.6.cloned.1.call-update
  66.6 0.0 all-gather.4.cloned.1.call-start
  66.6 69.7 %reduce-scatter.2.cloned.1.call-done = f32[512,256]{1,0:T(8,128)} async-done(((f32[512,4096]{1,0:T(8,128)}), f32[512,256]{1,0:T(8,128)}) %reduce-scatter.2.cloned.1.call-update) | async-done | bytes 524304 | tf_op jit(solution)/shard_map/reduce_scatter | solution.py:34
  136.3 1.8 multiply_convert_fusion
  138.1 0.0 all-gather.4.cloned.1.call-update
  138.1 10.5 %all-gather.6.cloned.1.call-done = bf16[4096,256]{1,0:T(8,128)(2,1)} async-done(((bf16[512,256]{1,0:T(8,128)(2,1)}), bf16[4096,256]{1,0:T(8,128)(2,1)}) %all-gather.6.cloned.1.call-update) | async-done | bytes 2097168 | tf_op jit(solution)/shard_map/all_gather | solution.py:36
  148.6 39.8 %all_to_all.19 = bf16[16,256,256]{2,1,0:T(8,128)(2,1)S(1)} all-to-all(bf16[16,256,256]{2,1,0:T(8,128)(2,1)} %bitcast.11), channel_id=1, replica_groups=mesh['coord'=16,'ex'=8] {'coord'}, dimensions={0} | all-to-all | bytes 4194304 | tf_op jit(solution)/shard_map/all_to_all | solution.py:37
  188.4 2.4 %copy.6 = bf16[256,16,256]{0,2,1:T(8,128)(2,1)} copy(bf16[256,16,256]{2,0,1:T(8,128)(2,1)S(1)} %bitcast.10) | data formatting | bytes 4194304 | tf_op jit(solution)/shard_map/all_to_all | solution.py:37
  190.7 18.3 %all-gather.4.cloned.1.call-done = bf16[512,4096]{1,0:T(8,128)(2,1)} async-done(((bf16[512,256]{1,0:T(8,128)(2,1)}), bf16[512,4096]{1,0:T(8,128)(2,1)}) %all-gather.4.cloned.1.call-update) | async-done | bytes 4194320 | tf_op jit(solution)/shard_map/all_gather | solution.py:35
  209.0 4.9 %fusion.24 = f32[512,256]{1,0:T(8,128)} fusion(bf16[512,4096]{1,0:T(8,128)(2,1)} %all-gather.4.cloned.1.call-done, bf16[256,4096]{0,1:T(8,128)(2,1)} %bitcast.12), kind=kOutput, calls=%fused_computation.39 | convolution fusion | flops 1073741824 | bytes 6815744 | tf_op jit(solution)/shard_map/dot_general | solution.py:38
  (1 shorter events, 0.0 us)
Async XLA Ops:
  7.4 129.0 %reduce-scatter.2.cloned.1.call-start = ((), (), s32[]{:S(2)}) async-start(), calls=%async_computation.2 | async-start | bytes 8912896 | tf_op jit(solution)/shard_map/reduce_scatter | solution.py:34
  31.3 11.7 %copy-start = (bf16[512,4096]{1,0:T(8,128)(2,1)S(1)}, bf16[512,4096]{1,0:T(8,128)(2,1)}, u32[]{:S(2)}) copy-start(bf16[512,4096]{1,0:T(8,128)(2,1)} %param.4) | copy-start | bytes 12582916
  66.0 82.6 %all-gather.6.cloned.1.call-start = ((), (), s32[]{:S(2)}) async-start(), calls=%async_computation.4 | async-start | bytes 2359296 | tf_op jit(solution)/shard_map/all_gather | solution.py:36
  66.6 142.4 %all-gather.4.cloned.1.call-start = ((), (), s32[]{:S(2)}) async-start(), calls=%async_computation.3 | async-start | bytes 4456448 | tf_op jit(solution)/shard_map/all_gather | solution.py:35
Sparse Core Ops, SparseCore 0:
  66.1 70.1 reduce-scatter.1
Sparse Core Ops, SparseCore 1:
  68.8 79.7 all-gather.5
  150.1 58.8 all-gather.3

commit v2 on v1

v2 whole, which is shorter than its diff:
```python
import functools
import math

import jax
import jax.numpy as jnp
from jax import lax
from jax.experimental import pallas as pl
from jax.experimental.pallas import tpu as pltpu
from jax.sharding import PartitionSpec as P

MESH = pl.DeviceIdType.MESH
CHUNKS = 4
ROWS = 128
SEG = 256
INNER = 128
OUTER = 32
CHIPS = 8
RING = 4
F32 = jnp.float32
BF16 = jnp.bfloat16


def kernel(
    scale,
    grad_ref, flip_ref, off_ref, query_ref, out_ref,
    own_g, sib_g, own_flip, sib_flip, off_buf, off_smem, table, signs, image,
    picks, x1_out, x1_in, x2_out, x2_in, mid, own_x, y_out, y_in, sketch, part_out, part_in, qbuf,
    gl_sem, gs_sem, gr_sem, fs_sem, fr_sem, os_sem, or_sem, om_sem,
    x1s_sem, x1r_sem, x2s_sem, x2r_sem, ys_sem, yr_sem, as_sem, ar_sem, ps_sem, pr_sem,
    qs_sem, qr_sem, zs_sem, zr_sem,
):
    c = lax.axis_index("coord")
    e = lax.axis_index("ex")
    core = lax.rem(c, 2)
    k = lax.div(c, 2)
    x = lax.rem(k, RING)
    y = lax.div(k, RING)
    z = lax.rem(e, RING)
    yh = lax.div(e, RING)

    def chip(yy, xx):
        return yy * RING + xx

    def coord(chip_index):
        return chip_index * 2 + core

    sib = c + 1 - 2 * core
    right = lax.rem(x + 1, RING)
    left = lax.rem(x + 3, RING)
    far = lax.rem(x + 2, RING)
    xr, xl = coord(chip(y, right)), coord(chip(y, left))
    yn = coord(chip(1 - y, x))
    zr = yh * RING + lax.rem(z + 1, RING)
    zl = yh * RING + lax.rem(z + 3, RING)

    def to_coord(src, dst, ssem, rsem, who):
        return pltpu.make_async_remote_copy(
            src_ref=src, dst_ref=dst, send_sem=ssem, recv_sem=rsem,
            device_id={"coord": who}, device_id_type=MESH)

    def to_dev(src, dst, ssem, rsem, who, where):
        return pltpu.make_async_remote_copy(
            src_ref=src, dst_ref=dst, send_sem=ssem, recv_sem=rsem,
            device_id={"coord": who, "ex": where}, device_id_type=MESH)

    bar = pltpu.get_barrier_semaphore()

    def greet(who, where):
        pl.semaphore_signal(bar, inc=1, device_id={"coord": who, "ex": where}, device_id_type=MESH)

    greet(sib, e)
    greet(c, zr)
    greet(c, zl)
    for d in range(1, CHIPS):
        greet(coord(lax.rem(k + d, CHIPS)), e)
    for d in range(CHIPS):
        @pl.when(jnp.logical_or(e != k, e != d))
        def _():
            greet(coord(e), d)
        @pl.when(jnp.logical_or(e != k, k != d))
        def _():
            greet(coord(d), k)
    own_copies = []
    for q in range(CHUNKS):
        own_copies.append(pltpu.make_async_copy(grad_ref.at[pl.ds(q * ROWS, ROWS)], own_g.at[q], gl_sem.at[q]))
        own_copies[q].start()
    @pl.when(e == k)
    def _():
        pl.semaphore_wait(bar, 10 + 14)
    @pl.when(e != k)
    def _():
        pl.semaphore_wait(bar, 10 + 16)

    sends = []

    def go(copy):
        copy.start()
        sends.append(copy)
        return copy

    go(to_coord(flip_ref, sib_flip, fs_sem, fr_sem, sib))
    grad_copies = []
    grad_copies.append(go(to_coord(grad_ref.at[pl.ds(0, ROWS)], sib_g.at[0], gs_sem.at[0], gr_sem.at[0], sib)))
    for d in range(1, CHIPS):
        go(to_coord(off_ref, off_buf.at[k], os_sem.at[d], or_sem.at[k], coord(lax.rem(k + d, CHIPS))))
    own_off = pltpu.make_async_copy(off_ref, off_buf.at[k], or_sem.at[k])
    own_off.start()
    for q in range(1, CHUNKS):
        grad_copies.append(go(to_coord(grad_ref.at[pl.ds(q * ROWS, ROWS)], sib_g.at[q], gs_sem.at[q], gr_sem.at[q], sib)))
    for d in range(CHIPS):
        dz, dy = d % RING, d // RING
        piece = query_ref.at[pl.ds(dz * ROWS, ROWS)]
        here = jnp.logical_and(e == k, e == d)
        @pl.when(here)
        def _():
            pltpu.make_async_copy(piece, qbuf.at[dz, k], qr_sem.at[k]).start()
        @pl.when(jnp.logical_not(here))
        def _():
            to_dev(piece, qbuf.at[dz, k], qs_sem.at[d], qr_sem.at[k], coord(e), d).start()

    row = lax.broadcasted_iota(jnp.int32, (INNER, 2 * INNER), 0)
    col = lax.rem(lax.broadcasted_iota(jnp.int32, (INNER, 2 * INNER), 1), INNER)
    both = row & col
    both = both ^ (both >> 4)
    both = both ^ (both >> 2)
    both = both ^ (both >> 1)
    table[...] = (1 - 2 * (both & 1)).astype(F32).astype(BF16)
    signs[:, 0:INNER] = ((1 - 2 * flip_ref[...]).astype(F32) * (1 - 2 * core).astype(F32)).astype(BF16)
    to_coord(flip_ref, sib_flip, fs_sem, fr_sem, sib).wait_recv()
    signs[:, INNER:] = (1 - 2 * sib_flip[...]).astype(F32).astype(BF16)

    def transform(q):
        own_copies[q].wait()
        grad_copies[q].wait_recv()
        for a in range(OUTER):
            weight = table[...] * signs[a:a + 1, :]
            data = jnp.concatenate(
                [own_g[q, :, a * INNER:(a + 1) * INNER], sib_g[q, :, a * INNER:(a + 1) * INNER]], axis=1)
            image[a * INNER:(a + 1) * INNER, :] = lax.dot_general(
                weight, data, (((1,), (1,)), ((), ())), preferred_element_type=F32)

        @pl.loop(0, INNER // 8)
        def _(t):
            base = pl.multiple_of(t * 8, 8)
            vals = [image[pl.ds(a * INNER + base, 8), :] for a in range(OUTER)]
            h = 1
            while h < OUTER:
                vals = [vals[a] + vals[a + h] if not a & h else vals[a - h] - vals[a] for a in range(OUTER)]
                h *= 2
            for a in range(OUTER):
                image[pl.ds(a * INNER + base, 8), :] = vals[a]

    def pick(yy, xx, dst):
        seg = chip(yy, xx)

        @pl.loop(0, SEG // 32)
        def _(t):
            base = pl.multiple_of(t * 32, 32)
            for u in range(32):
                dst[pl.ds(base + u, 1), :] = image[pl.ds(off_smem[seg, 0, base + u], 1), :]

    def sign_of(yy, xx):
        odd = lax.rem(xx, 2) * lax.rem(x, 2) + lax.div(xx, 2) * lax.div(x, 2) + yy * y
        return (1 - 2 * lax.rem(odd, 2)).astype(F32)

    x1 = {}
    x2 = {}
    yc = {}
    ac = {}
    pc = {}

    def first_picks(q):
        for d in range(2):
            pick(d, far, picks)
            x1_out[q, d] = (picks[...] * sign_of(d, far)).astype(BF16)
            x1[q, d] = go(to_coord(x1_out.at[q, d], x1_in.at[q, d], x1s_sem.at[q, d], x1r_sem.at[q, d], (xr, xl)[d]))

    def send2(q, d, yy):
        x2[q, d, yy] = go(to_coord(
            x2_out.at[q, d, yy], x2_in.at[q, d, yy], x2s_sem.at[q, d, yy], x2r_sem.at[q, d, yy], (xr, xl)[d]))

    def other_picks(q):
        for d in range(2):
            xx = (right, left)[d]
            pick(1 - d, xx, picks)
            x2_out[q, d, 1 - d] = (picks[...] * sign_of(1 - d, xx)).astype(BF16)
            send2(q, d, 1 - d)
        for d in range(2):
            pick(d, (right, left)[d], mid.at[q, d])
        for yy in range(2):
            pick(yy, x, own_x.at[q, yy])

    def compute(q):
        transform(q)
        if q == 0:
            own_off.wait()
            for d in range(1, CHIPS):
                s = lax.rem(k + d, CHIPS)
                to_coord(off_ref, off_buf.at[s], os_sem.at[d], or_sem.at[s], coord(s)).wait_recv()
            om = pltpu.make_async_copy(off_buf, off_smem, om_sem)
            om.start()
            om.wait()
        first_picks(q)
        other_picks(q)

    def combine_x(q):
        for d in range(2):
            x1[q, d].wait_recv()
            x2_out[q, d, d] = (mid[q, d] * sign_of(d, (right, left)[d]) + x1_in[q, d].astype(F32)).astype(BF16)
            send2(q, d, d)

    def reduce_x(q):
        for d in range(2):
            for yy in range(2):
                x2[q, d, yy].wait_recv()
        there = 1 - y
        y_out[q] = (own_x[q, there] * sign_of(there, x)
                    + (x2_in[q, 0, there].astype(F32) + x2_in[q, 1, there].astype(F32)))
        yc[q] = go(to_coord(y_out.at[q], y_in.at[q], ys_sem.at[q], yr_sem.at[q], yn))
        own_x[q, y] = (own_x[q, y] * sign_of(y, x)
                       + (x2_in[q, 0, y].astype(F32) + x2_in[q, 1, y].astype(F32)))

    def gather_send(q, slot, n, who):
        return go(to_coord(sketch.at[q, slot], sketch.at[q, slot], as_sem.at[q, n], ar_sem.at[q, slot], who))

    def gather_wait(q, slot):
        to_coord(sketch.at[q, slot], sketch.at[q, slot], as_sem.at[q, 0], ar_sem.at[q, slot], sib).wait_recv()

    def make_sketch(q):
        yc[q].wait_recv()
        total = (own_x[q, y] + y_in[q]) * scale
        sketch[q, k] = total.T.astype(BF16)
        gather_send(q, k, 0, yn)
        gather_send(q, k, 1, xr)
        gather_send(q, k, 2, xl)

    def gather_y(q):
        slot = chip(1 - y, x)
        gather_wait(q, slot)
        gather_send(q, slot, 3, xr)
        gather_send(q, slot, 4, xl)

    def gather_x(q):
        gather_wait(q, chip(0, left))
        gather_send(q, chip(0, left), 5, xr)
        gather_wait(q, chip(1, right))
        gather_send(q, chip(1, right), 6, xl)

    def score(q):
        gather_wait(q, chip(1, left))
        gather_wait(q, chip(0, right))
        gather_wait(q, chip(0, far))
        gather_wait(q, chip(1, far))

        def half(first):
            total = None
            for s in range(CHIPS):
                rhs = jnp.concatenate([qbuf[first, s], qbuf[first + 1, s]], axis=0)
                term = lax.dot_general(sketch[q, s], rhs, (((1,), (1,)), ((), ())), preferred_element_type=F32)
                total = term if total is None else total + term
            return total

        part_out[q] = half(2 - 2 * core)
        pc[q] = go(to_coord(part_out.at[q], part_in.at[q], ps_sem.at[q], pr_sem.at[q], sib))
        out_ref[q * ROWS:(q + 1) * ROWS, :] = half(2 * core)

    def finish(q):
        pc[q].wait_recv()
        out_ref[q * ROWS:(q + 1) * ROWS, :] = out_ref[q * ROWS:(q + 1) * ROWS, :] + part_in[q]

    zw = RING * 2

    def query_ring():
        for s in range(CHIPS):
            pltpu.make_async_copy(qbuf.at[z, s], qbuf.at[z, s], qr_sem.at[s]).wait()
        go(to_dev(qbuf.at[z], qbuf.at[z], zs_sem.at[0], zr_sem.at[0], c, zr))
        go(to_dev(qbuf.at[z], qbuf.at[z], zs_sem.at[1], zr_sem.at[1], c, zl))

    half_q = CHIPS // 2

    def query_forward():
        a = lax.rem(z + 3, RING)
        b = lax.rem(z + 1, RING)
        f = lax.rem(z + 2, RING)
        to_dev(qbuf.at[a], qbuf.at[a], zs_sem.at[0], zr_sem.at[0], c, zr).wait_recv()
        lo = qbuf.at[a, pl.ds(0, half_q)]
        go(to_dev(lo, lo, zs_sem.at[2], zr_sem.at[2], c, zr))
        to_dev(qbuf.at[b], qbuf.at[b], zs_sem.at[1], zr_sem.at[1], c, zl).wait_recv()
        hi = qbuf.at[b, pl.ds(half_q, half_q)]
        go(to_dev(hi, hi, zs_sem.at[3], zr_sem.at[3], c, zl))

    def query_done():
        f = lax.rem(z + 2, RING)
        lo = qbuf.at[f, pl.ds(0, half_q)]
        to_dev(lo, lo, zs_sem.at[2], zr_sem.at[2], c, zr).wait_recv()
        hi = qbuf.at[f, pl.ds(half_q, half_q)]
        to_dev(hi, hi, zs_sem.at[3], zr_sem.at[3], c, zl).wait_recv()

    compute(0)
    query_ring()
    combine_x(0)
    compute(1)
    reduce_x(0)
    combine_x(1)
    query_forward()
    make_sketch(0)
    compute(2)
    reduce_x(1)
    gather_y(0)
    combine_x(2)
    make_sketch(1)
    gather_x(0)
    compute(3)
    reduce_x(2)
    gather_y(1)
    combine_x(3)
    make_sketch(2)
    query_done()
    score(0)
    gather_x(1)
    reduce_x(3)
    gather_y(2)
    make_sketch(3)
    score(1)
    finish(0)
    gather_x(2)
    gather_y(3)
    score(2)
    finish(1)
    gather_x(3)
    score(3)
    finish(2)
    finish(3)

    for copy in sends:
        copy.wait_send()
    for d in range(CHIPS):
        dz = d % RING
        @pl.when(jnp.logical_not(jnp.logical_and(e == k, e == d)))
        def _():
            to_dev(query_ref.at[pl.ds(dz * ROWS, ROWS)], qbuf.at[dz, k], qs_sem.at[d], qr_sem.at[k], coord(e), d).wait_send()


def body(gradients, sign_flips, pick_offsets, queries):
    rows, width = gradients.shape
    scale = 1.0 / math.sqrt(width * lax.axis_size("coord"))
    dma = pltpu.SemaphoreType.DMA
    vmem = pltpu.VMEM
    block = (SEG, ROWS)
    return pl.pallas_call(
        functools.partial(kernel, scale),
        out_shape=jax.ShapeDtypeStruct((rows, queries.shape[1]), F32),
        in_specs=[
            pl.BlockSpec(memory_space=pl.ANY),
            pl.BlockSpec(memory_space=pltpu.VMEM),
            pl.BlockSpec(memory_space=pltpu.VMEM),
            pl.BlockSpec(memory_space=pltpu.VMEM),
        ],
        out_specs=pl.BlockSpec(memory_space=pltpu.VMEM),
        scratch_shapes=[
            vmem((CHUNKS, ROWS, width), BF16),
            vmem((CHUNKS, ROWS, width), BF16),
            vmem((OUTER, INNER), jnp.int32),
            vmem((OUTER, INNER), jnp.int32),
            vmem((CHIPS, 1, SEG), jnp.int32),
            pltpu.SMEM((CHIPS, 1, SEG), jnp.int32),
            vmem((INNER, 2 * INNER), BF16),
            vmem((OUTER, 2 * INNER), BF16),
            vmem((width, ROWS), F32),
            vmem(block, F32),
            vmem((CHUNKS, 2) + block, BF16),
            vmem((CHUNKS, 2) + block, BF16),
            vmem((CHUNKS, 2, 2) + block, BF16),
            vmem((CHUNKS, 2, 2) + block, BF16),
            vmem((CHUNKS, 2) + block, F32),
            vmem((CHUNKS, 2) + block, F32),
            vmem((CHUNKS,) + block, F32),
            vmem((CHUNKS,) + block, F32),
            vmem((CHUNKS, CHIPS, ROWS, SEG), BF16),
            vmem((CHUNKS, ROWS, 256), F32),
            vmem((CHUNKS, ROWS, 256), F32),
            vmem((RING, CHIPS, ROWS, SEG), BF16),
            dma((CHUNKS,)), dma((CHUNKS,)), dma((CHUNKS,)),
            dma(()), dma(()),
            dma((CHIPS,)), dma((CHIPS,)), dma(()),
            dma((CHUNKS, 2)), dma((CHUNKS, 2)),
            dma((CHUNKS, 2, 2)), dma((CHUNKS, 2, 2)),
            dma((CHUNKS,)), dma((CHUNKS,)),
            dma((CHUNKS, 7)), dma((CHUNKS, CHIPS)),
            dma((CHUNKS,)), dma((CHUNKS,)),
            dma((CHIPS,)), dma((CHIPS,)), dma((4,)), dma((4,)),
        ],
        compiler_params=pltpu.CompilerParams(
            collective_id=0, has_side_effects=True, vmem_limit_bytes=56 << 20),
    )(gradients, sign_flips.reshape(OUTER, INNER), pick_offsets.reshape(1, SEG), queries)


def solution(mesh):
    in_specs = (P("ex", "coord"), P("coord"), P("coord"), P("ex", "coord"))
    return jax.shard_map(body, mesh=mesh, in_specs=in_specs, out_specs=P("ex", "coord"), check_vma=False)
```

time: 222 us -> 115 us (0.52)
  Pallas kernels: 0 us -> 113 us
  waiting for transfers between devices: 99 us -> 0 us
  blocking collectives: 61 us -> 0 us
  matrix products: 27.9 us -> 0 us
  other arithmetic: 16.1 us -> 0 us
  between operations: 14.9 us -> 0.01 us
    pallas_call x0 -> x1, Pallas kernels: none -> 113 us  [body(): pl.pallas_call(functools.partial(kernel, scale), out_shape=jax.ShapeDtype...]
    reduce_scatter x1 -> x0, waiting for transfers between devices: 69.7 us -> none  [body(): lax.psum_scatter(partial, 'coord', scatter_dimension=1, tiled=True) * scale]
    all_to_all x1 -> x0, blocking collectives: 39.8 us -> none  [body(): lax.all_to_all(mine, 'coord', split_axis=0, concat_axis=1, tiled=True)]
    all_gather x2 -> x0, waiting for transfers between devices: 28.7 us -> none  [the longest x1 18.3 us: body(): lax.all_gather(picked.astype(jnp.bfloat16), 'coord', axis=1, tiled=True)]
    dot_general x2 -> x0, matrix products: 27.9 us -> none  [the longest x1 23 us: body(): partial = jnp.dot(signed, table, preferred_element_type=jnp.float32)]
    all_gather x1 -> x0, blocking collectives: 21.2 us -> none  [body(): offsets = lax.all_gather(pick_offsets, 'coord', axis=0, tiled=True)]
    mul x2 -> x0, other arithmetic: 12 us -> none  [body(): table = (high * far[None, :])[:, None, :] * low[None, :, :]]
    convert_element_type x3 -> x0, other arithmetic: 4.1 us -> none  [the longest x1 1.78 us: body(): picked.astype(jnp.bfloat16)]
  transfers between devices with their start and end apart: 3 -> 0, of which waited for: 3 -> 0; matrix products, arithmetic and copies ran while one was open for 2% -> 0% of each run, Pallas kernels for 0% -> 0%
where the time goes in v2:
time: 115 us
  Pallas kernels  113 us (98%)
  local copies, waits for them, and re-layouts  1.87 us (2%)
    pallas_call x1, Pallas kernels, body(): pl.pallas_call(functools.partial(kernel, scale), out_shape=jax.ShapeDtype...  113 us

profile of v2, /device:TPU:1, one launch (start us, length us, event | category | flops | bytes accessed | tf_op | source)
XLA Modules:
  0.0 114.8 jit_solution(8575411910691288222)
XLA Ops:
  0.0 113.0 %shard_map.46 = f32[512,256]{1,0:T(8,128)} custom-call(bf16[512,4096]{1,0:T(8,128)(2,1)} %grad_ref.1, s32[32,128]{1,0:T(8,128)} %bitcast.2, s32[1,256]{1,0:T(1,128)} %bitcast.3, bf16[512,256]{1,0:T(8,128)(2,1)} %query_ref.1), custom_call_target="tpu_custom_call" | custom-call | tf_op jit(solution)/shard_map/pallas_call | solution.py:350
  113.0 1.9 %copy.6 = f32[512,256]{1,0:T(8,128)} copy(f32[512,256]{1,0:T(8,128)} %shard_map.46) | data formatting | bytes 1048576

commit v3 on v2

--- a/solution.py
+++ b/solution.py
@@ -18,16 +18,23 @@
 RING = 4
 F32 = jnp.float32
 BF16 = jnp.bfloat16
+ORDER = (
+    "T0q0A0B0C0D0T1A1B1C1X0D1",
+    "T2A2X1B2r0C2D2T3R0A3X2B3",
+    "R1C3D3S0X3R2S1y0b0a0w0R3",
+    "S2b1a1y1f0b2a2f1S3d0f2y2",
+    "b3a3M0f3F0M1y3F1M2F2M3F3",
+)
 
 
 def kernel(
     scale,
     grad_ref, flip_ref, off_ref, query_ref, out_ref,
     own_g, sib_g, own_flip, sib_flip, off_buf, off_smem, table, signs, image,
-    picks, x1_out, x1_in, x2_out, x2_in, mid, own_x, y_out, y_in, sketch, part_out, part_in, qbuf,
+    picks, x1_out, x1_in, x2_out, x2_in, mid, own_x, y_out, y_in, sketch, part_out, part_in, abuf, qbuf,
     gl_sem, gs_sem, gr_sem, fs_sem, fr_sem, os_sem, or_sem, om_sem,
     x1s_sem, x1r_sem, x2s_sem, x2r_sem, ys_sem, yr_sem, as_sem, ar_sem, ps_sem, pr_sem,
-    qs_sem, qr_sem, zs_sem, zr_sem,
+    qas_sem, qar_sem, qs_sem, qr_sem, zs_sem, zr_sem,
 ):
     c = lax.axis_index("coord")
     e = lax.axis_index("ex")
@@ -49,6 +56,9 @@
     left = lax.rem(x + 3, RING)
     far = lax.rem(x + 2, RING)
     xr, xl = coord(chip(y, right)), coord(chip(y, left))
+    ahead = lax.rem(x + 1 + 2 * y, RING)
+    behind = lax.rem(x + 3 + 2 * y, RING)
+    xa, xb = coord(chip(y, ahead)), coord(chip(y, behind))
     yn = coord(chip(1 - y, x))
     zr = yh * RING + lax.rem(z + 1, RING)
     zl = yh * RING + lax.rem(z + 3, RING)
@@ -69,27 +79,37 @@
         pl.semaphore_signal(bar, inc=1, device_id={"coord": who, "ex": where}, device_id_type=MESH)
 
     greet(sib, e)
-    greet(c, zr)
-    greet(c, zl)
+    for d in range(1, RING):
+        greet(c, yh * RING + lax.rem(z + d, RING))
     for d in range(1, CHIPS):
         greet(coord(lax.rem(k + d, CHIPS)), e)
     for d in range(CHIPS):
-        @pl.when(jnp.logical_or(e != k, e != d))
+        dz, dy = d % RING, d // RING
+        @pl.when(jnp.logical_or(y != yh, jnp.logical_or(x != dz, dy != yh)))
         def _():
-            greet(coord(e), d)
-        @pl.when(jnp.logical_or(e != k, k != d))
+            greet(coord(chip(yh, dz)), dy * RING + z)
+        @pl.when(jnp.logical_or(y != yh, k != d))
         def _():
-            greet(coord(d), k)
+            greet(coord(d), y * RING + z)
     own_copies = []
     for q in range(CHUNKS):
         own_copies.append(pltpu.make_async_copy(grad_ref.at[pl.ds(q * ROWS, ROWS)], own_g.at[q], gl_sem.at[q]))
         own_copies[q].start()
-    @pl.when(e == k)
+    row = lax.broadcasted_iota(jnp.int32, (INNER, 2 * INNER), 0)
+    col = lax.rem(lax.broadcasted_iota(jnp.int32, (INNER, 2 * INNER), 1), INNER)
+    both = row & col
+    both = both ^ (both >> 4)
+    both = both ^ (both >> 2)
+    both = both ^ (both >> 1)
+    table[...] = (1 - 2 * (both & 1)).astype(F32).astype(BF16)
+    signs[:, 0:INNER] = ((1 - 2 * flip_ref[...]).astype(F32) * (1 - 2 * core).astype(F32)).astype(BF16)
+
+    @pl.when(y == yh)
     def _():
-        pl.semaphore_wait(bar, 10 + 14)
-    @pl.when(e != k)
+        pl.semaphore_wait(bar, 11 + 14)
+    @pl.when(y != yh)
     def _():
-        pl.semaphore_wait(bar, 10 + 16)
+        pl.semaphore_wait(bar, 11 + 16)
 
     sends = []
 
@@ -107,25 +127,11 @@
     own_off.start()
     for q in range(1, CHUNKS):
         grad_copies.append(go(to_coord(grad_ref.at[pl.ds(q * ROWS, ROWS)], sib_g.at[q], gs_sem.at[q], gr_sem.at[q], sib)))
-    for d in range(CHIPS):
-        dz, dy = d % RING, d // RING
-        piece = query_ref.at[pl.ds(dz * ROWS, ROWS)]
-        here = jnp.logical_and(e == k, e == d)
-        @pl.when(here)
-        def _():
-            pltpu.make_async_copy(piece, qbuf.at[dz, k], qr_sem.at[k]).start()
-        @pl.when(jnp.logical_not(here))
-        def _():
-            to_dev(piece, qbuf.at[dz, k], qs_sem.at[d], qr_sem.at[k], coord(e), d).start()
-
-    row = lax.broadcasted_iota(jnp.int32, (INNER, 2 * INNER), 0)
-    col = lax.rem(lax.broadcasted_iota(jnp.int32, (INNER, 2 * INNER), 1), INNER)
-    both = row & col
-    both = both ^ (both >> 4)
-    both = both ^ (both >> 2)
-    both = both ^ (both >> 1)
-    table[...] = (1 - 2 * (both & 1)).astype(F32).astype(BF16)
-    signs[:, 0:INNER] = ((1 - 2 * flip_ref[...]).astype(F32) * (1 - 2 * core).astype(F32)).astype(BF16)
+    pltpu.make_async_copy(query_ref.at[pl.ds(z * ROWS, ROWS)], abuf.at[z], qar_sem.at[z]).start()
+    for d in (1, 3, 2):
+        zt = lax.rem(z + d, RING)
+        go(to_dev(query_ref.at[pl.ds(zt * ROWS, ROWS)], abuf.at[z], qas_sem.at[d], qar_sem.at[z], c, yh * RING + zt))
+
     to_coord(flip_ref, sib_flip, fs_sem, fr_sem, sib).wait_recv()
     signs[:, INNER:] = (1 - 2 * sib_flip[...]).astype(F32).astype(BF16)
 
@@ -170,28 +176,6 @@
     pc = {}
 
     def first_picks(q):
-        for d in range(2):
-            pick(d, far, picks)
-            x1_out[q, d] = (picks[...] * sign_of(d, far)).astype(BF16)
-            x1[q, d] = go(to_coord(x1_out.at[q, d], x1_in.at[q, d], x1s_sem.at[q, d], x1r_sem.at[q, d], (xr, xl)[d]))
-
-    def send2(q, d, yy):
-        x2[q, d, yy] = go(to_coord(
-            x2_out.at[q, d, yy], x2_in.at[q, d, yy], x2s_sem.at[q, d, yy], x2r_sem.at[q, d, yy], (xr, xl)[d]))
-
-    def other_picks(q):
-        for d in range(2):
-            xx = (right, left)[d]
-            pick(1 - d, xx, picks)
-            x2_out[q, d, 1 - d] = (picks[...] * sign_of(1 - d, xx)).astype(BF16)
-            send2(q, d, 1 - d)
-        for d in range(2):
-            pick(d, (right, left)[d], mid.at[q, d])
-        for yy in range(2):
-            pick(yy, x, own_x.at[q, yy])
-
-    def compute(q):
-        transform(q)
         if q == 0:
             own_off.wait()
             for d in range(1, CHIPS):
@@ -200,8 +184,29 @@
             om = pltpu.make_async_copy(off_buf, off_smem, om_sem)
             om.start()
             om.wait()
-        first_picks(q)
-        other_picks(q)
+        for d in range(2):
+            pick(d, far, picks)
+            x1_out[q, d] = (picks[...] * sign_of(d, far)).astype(BF16)
+            x1[q, d] = go(to_coord(x1_out.at[q, d], x1_in.at[q, d], x1s_sem.at[q, d], x1r_sem.at[q, d], (xr, xl)[d]))
+
+    def send2(q, d, yy):
+        x2[q, d, yy] = go(to_coord(
+            x2_out.at[q, d, yy], x2_in.at[q, d, yy], x2s_sem.at[q, d, yy], x2r_sem.at[q, d, yy], (xr, xl)[d]))
+
+    def single_picks(q):
+        for d in range(2):
+            xx = (right, left)[d]
+            pick(1 - d, xx, picks)
+            x2_out[q, d, 1 - d] = (picks[...] * sign_of(1 - d, xx)).astype(BF16)
+            send2(q, d, 1 - d)
+
+    def mid_picks(q):
+        for d in range(2):
+            pick(d, (right, left)[d], mid.at[q, d])
+
+    def own_picks(q):
+        for yy in range(2):
+            pick(yy, x, own_x.at[q, yy])
 
     def combine_x(q):
         for d in range(2):
@@ -231,26 +236,33 @@
         total = (own_x[q, y] + y_in[q]) * scale
         sketch[q, k] = total.T.astype(BF16)
         gather_send(q, k, 0, yn)
-        gather_send(q, k, 1, xr)
-        gather_send(q, k, 2, xl)
+        gather_send(q, k, 1, xa)
+        gather_send(q, k, 2, xb)
+
+    def gather_behind(q):
+        slot = chip(y, behind)
+        gather_wait(q, slot)
+        gather_send(q, slot, 3, xa)
+
+    def gather_ahead(q):
+        slot = chip(y, ahead)
+        gather_wait(q, slot)
+        gather_send(q, slot, 4, yn)
 
     def gather_y(q):
         slot = chip(1 - y, x)
         gather_wait(q, slot)
-        gather_send(q, slot, 3, xr)
-        gather_send(q, slot, 4, xl)
-
-    def gather_x(q):
-        gather_wait(q, chip(0, left))
-        gather_send(q, chip(0, left), 5, xr)
-        gather_wait(q, chip(1, right))
-        gather_send(q, chip(1, right), 6, xl)
+        gather_send(q, slot, 5, xb)
+
+    def gather_far(q):
+        slot = chip(y, far)
+        gather_wait(q, slot)
+        gather_send(q, slot, 6, yn)
 
     def score(q):
-        gather_wait(q, chip(1, left))
-        gather_wait(q, chip(0, right))
-        gather_wait(q, chip(0, far))
-        gather_wait(q, chip(1, far))
+        gather_wait(q, chip(1 - y, right))
+        gather_wait(q, chip(1 - y, left))
+        gather_wait(q, chip(1 - y, far))
 
         def half(first):
             total = None
@@ -268,9 +280,21 @@
         pc[q].wait_recv()
         out_ref[q * ROWS:(q + 1) * ROWS, :] = out_ref[q * ROWS:(q + 1) * ROWS, :] + part_in[q]
 
-    zw = RING * 2
-
-    def query_ring():
+    def query_spread(_):
+        for dz in range(RING):
+            pltpu.make_async_copy(abuf.at[dz], abuf.at[dz], qar_sem.at[dz]).wait()
+            for dy in range(2):
+                d = dy * RING + dz
+                here = jnp.logical_and(y == yh, jnp.logical_and(x == dz, dy == yh))
+                @pl.when(here)
+                def _():
+                    pltpu.make_async_copy(abuf.at[dz], qbuf.at[z, k], qr_sem.at[k]).start()
+                @pl.when(jnp.logical_not(here))
+                def _():
+                    to_dev(abuf.at[dz], qbuf.at[z, k], qs_sem.at[d], qr_sem.at[k],
+                           coord(chip(yh, dz)), dy * RING + z).start()
+
+    def query_ring(_):
         for s in range(CHIPS):
             pltpu.make_async_copy(qbuf.at[z, s], qbuf.at[z, s], qr_sem.at[s]).wait()
         go(to_dev(qbuf.at[z], qbuf.at[z], zs_sem.at[0], zr_sem.at[0], c, zr))
@@ -278,7 +302,7 @@
 
     half_q = CHIPS // 2
 
-    def query_forward():
+    def query_forward(_):
         a = lax.rem(z + 3, RING)
         b = lax.rem(z + 1, RING)
         f = lax.rem(z + 2, RING)
@@ -289,56 +313,31 @@
         hi = qbuf.at[b, pl.ds(half_q, half_q)]
         go(to_dev(hi, hi, zs_sem.at[3], zr_sem.at[3], c, zl))
 
-    def query_done():
+    def query_done(_):
         f = lax.rem(z + 2, RING)
         lo = qbuf.at[f, pl.ds(0, half_q)]
         to_dev(lo, lo, zs_sem.at[2], zr_sem.at[2], c, zr).wait_recv()
         hi = qbuf.at[f, pl.ds(half_q, half_q)]
         to_dev(hi, hi, zs_sem.at[3], zr_sem.at[3], c, zl).wait_recv()
 
-    compute(0)
-    query_ring()
-    combine_x(0)
-    compute(1)
-    reduce_x(0)
-    combine_x(1)
-    query_forward()
-    make_sketch(0)
-    compute(2)
-    reduce_x(1)
-    gather_y(0)
-    combine_x(2)
-    make_sketch(1)
-    gather_x(0)
-    compute(3)
-    reduce_x(2)
-    gather_y(1)
-    combine_x(3)
-    make_sketch(2)
-    query_done()
-    score(0)
-    gather_x(1)
-    reduce_x(3)
-    gather_y(2)
-    make_sketch(3)
-    score(1)
-    finish(0)
-    gather_x(2)
-    gather_y(3)
-    score(2)
-    finish(1)
-    gather_x(3)
-    score(3)
-    finish(2)
-    finish(3)
+    ops = {
+        "T": transform, "A": first_picks, "B": single_picks, "C": mid_picks, "D": own_picks,
+        "X": combine_x, "R": reduce_x, "S": make_sketch,
+        "b": gather_behind, "a": gather_ahead, "y": gather_y, "f": gather_far,
+        "M": score, "F": finish, "q": query_spread, "r": query_ring, "w": query_forward, "d": query_done,
+    }
+    steps = "".join(ORDER)
+    for i in range(0, len(steps), 2):
+        ops[steps[i]](int(steps[i + 1]))
 
     for copy in sends:
         copy.wait_send()
     for d in range(CHIPS):
-        dz = d % RING
-        @pl.when(jnp.logical_not(jnp.logical_and(e == k, e == d)))
+        dz, dy = d % RING, d // RING
+        @pl.when(jnp.logical_or(y != yh, jnp.logical_or(x != dz, dy != yh)))
         def _():
-            to_dev(query_ref.at[pl.ds(dz * ROWS, ROWS)], qbuf.at[dz, k], qs_sem.at[d], qr_sem.at[k], coord(e), d).wait_send()
+            to_dev(abuf.at[dz], qbuf.at[z, k], qs_sem.at[d], qr_sem.at[k],
+                   coord(chip(yh, dz)), dy * RING + z).wait_send()
 
 
 def body(gradients, sign_flips, pick_offsets, queries):
@@ -354,7 +353,7 @@
             pl.BlockSpec(memory_space=pl.ANY),
             pl.BlockSpec(memory_space=pltpu.VMEM),
             pl.BlockSpec(memory_space=pltpu.VMEM),
-            pl.BlockSpec(memory_space=pltpu.VMEM),
+            pl.BlockSpec(memory_space=pl.ANY),
         ],
         out_specs=pl.BlockSpec(memory_space=pltpu.VMEM),
         scratch_shapes=[
@@ -379,6 +378,7 @@
             vmem((CHUNKS, CHIPS, ROWS, SEG), BF16),
             vmem((CHUNKS, ROWS, 256), F32),
             vmem((CHUNKS, ROWS, 256), F32),
+            vmem((RING, ROWS, SEG), BF16),
             vmem((RING, CHIPS, ROWS, SEG), BF16),
             dma((CHUNKS,)), dma((CHUNKS,)), dma((CHUNKS,)),
             dma(()), dma(()),
@@ -388,7 +388,7 @@
             dma((CHUNKS,)), dma((CHUNKS,)),
             dma((CHUNKS, 7)), dma((CHUNKS, CHIPS)),
             dma((CHUNKS,)), dma((CHUNKS,)),
-            dma((CHIPS,)), dma((CHIPS,)), dma((4,)), dma((4,)),
+            dma((RING,)), dma((RING,)), dma((CHIPS,)), dma((CHIPS,)), dma((4,)), dma((4,)),
         ],
         compiler_params=pltpu.CompilerParams(
             collective_id=0, has_side_effects=True, vmem_limit_bytes=56 << 20),

time: 115 us -> 69.7 us (0.61)
  Pallas kernels: 113 us -> 67.6 us
    pallas_call x1, Pallas kernels: 113 us -> 67.6 us  [body(): pl.pallas_call(functools.partial(kernel, scale), out_shape=jax.ShapeDtype...]
where the time goes in v3:
time: 69.7 us; the launch traced here: 69.5 us
  Pallas kernels  67.6 us (97%)
  local copies, waits for them, and re-layouts  1.87 us (3%)
    pallas_call x1, Pallas kernels, body(): pl.pallas_call(functools.partial(kernel, scale), out_shape=jax.ShapeDtype...  67.6 us
    unnamed x1, local copies, waits for them, and re-layouts  1.87 us

profile of v3, /device:TPU:1, one launch (start us, length us, event | category | flops | bytes accessed | tf_op | source)
XLA Modules:
  0.0 69.5 jit_solution(13048866147976815035)
XLA Ops:
  0.0 67.6 %shard_map.46 = f32[512,256]{1,0:T(8,128)} custom-call(bf16[512,4096]{1,0:T(8,128)(2,1)} %grad_ref.1, s32[32,128]{1,0:T(8,128)} %bitcast.2, s32[1,256]{1,0:T(1,128)} %bitcast.3, bf16[512,256]{1,0:T(8,128)(2,1)} %query_ref.1), custom_call_target="tpu_custom_call" | custom-call | tf_op jit(solution)/shard_map/pallas_call | solution.py:349
  67.6 1.9 %copy.6 = f32[512,256]{1,0:T(8,128)} copy(f32[512,256]{1,0:T(8,128)} %shard_map.46) | data formatting | bytes 1048576

commit v4 on v3

--- a/solution.py
+++ b/solution.py
@@ -19,7 +19,7 @@
 F32 = jnp.float32
 BF16 = jnp.bfloat16
 ORDER = (
-    "T0q0A0B0C0D0T1A1B1C1X0D1",
+    "T0A0q0B0C0D0T1A1B1C1X0D1",
     "T2A2X1B2r0C2D2T3R0A3X2B3",
     "R1C3D3S0X3R2S1y0b0a0w0R3",
     "S2b1a1y1f0b2a2f1S3d0f2y2",
@@ -159,10 +159,10 @@
     def pick(yy, xx, dst):
         seg = chip(yy, xx)
 
-        @pl.loop(0, SEG // 32)
+        @pl.loop(0, SEG // 64)
         def _(t):
-            base = pl.multiple_of(t * 32, 32)
-            for u in range(32):
+            base = pl.multiple_of(t * 64, 64)
+            for u in range(64):
                 dst[pl.ds(base + u, 1), :] = image[pl.ds(off_smem[seg, 0, base + u], 1), :]
 
     def sign_of(yy, xx):

time: 69.7 us -> 68.3 us (0.980)
  Pallas kernels: 67.6 us -> 66.2 us
    pallas_call x1, Pallas kernels: 67.6 us -> 66.2 us  [body(): pl.pallas_call(functools.partial(kernel, scale), out_shape=jax.ShapeDtype...]
where the time goes in v4:
time: 68.3 us; the launch traced here: 68.1 us
  Pallas kernels  66.2 us (97%)
  local copies, waits for them, and re-layouts  1.87 us (3%)
    pallas_call x1, Pallas kernels, body(): pl.pallas_call(functools.partial(kernel, scale), out_shape=jax.ShapeDtype...  66.2 us
    unnamed x1, local copies, waits for them, and re-layouts  1.87 us

profile of v4, /device:TPU:1, one launch (start us, length us, event | category | flops | bytes accessed | tf_op | source)
XLA Modules:
  0.0 68.1 jit_solution(13818454573277563236)
XLA Ops:
  0.0 66.2 %shard_map.46 = f32[512,256]{1,0:T(8,128)} custom-call(bf16[512,4096]{1,0:T(8,128)(2,1)} %grad_ref.1, s32[32,128]{1,0:T(8,128)} %bitcast.2, s32[1,256]{1,0:T(1,128)} %bitcast.3, bf16[512,256]{1,0:T(8,128)(2,1)} %query_ref.1), custom_call_target="tpu_custom_call" | custom-call | tf_op jit(solution)/shard_map/pallas_call | solution.py:349
  66.2 1.9 %copy.6 = f32[512,256]{1,0:T(8,128)} copy(f32[512,256]{1,0:T(8,128)} %shard_map.46) | data formatting | bytes 1048576

commit v5 on v4

--- a/solution.py
+++ b/solution.py
@@ -20,7 +20,7 @@
 BF16 = jnp.bfloat16
 ORDER = (
     "T0A0q0B0C0D0T1A1B1C1X0D1",
-    "T2A2X1B2r0C2D2T3R0A3X2B3",
+    "T2A2X1B2r0C2D2R0T3A3X2B3",
     "R1C3D3S0X3R2S1y0b0a0w0R3",
     "S2b1a1y1f0b2a2f1S3d0f2y2",
     "b3a3M0f3F0M1y3F1M2F2M3F3",

time: 68.3 us -> 68.3 us (level)
  no operation moved by 1% of the time
where the time goes in v5:
time: 68.3 us; the launch traced here: 68.1 us
  Pallas kernels  66.2 us (97%)
  local copies, waits for them, and re-layouts  1.87 us (3%)
    pallas_call x1, Pallas kernels, body(): pl.pallas_call(functools.partial(kernel, scale), out_shape=jax.ShapeDtype...  66.2 us
    unnamed x1, local copies, waits for them, and re-layouts  1.87 us

profile of v5, /device:TPU:1, one launch (start us, length us, event | category | flops | bytes accessed | tf_op | source)
XLA Modules:
  0.0 68.1 jit_solution(4497803690840698829)
XLA Ops:
  0.0 66.2 %shard_map.46 = f32[512,256]{1,0:T(8,128)} custom-call(bf16[512,4096]{1,0:T(8,128)(2,1)} %grad_ref.1, s32[32,128]{1,0:T(8,128)} %bitcast.2, s32[1,256]{1,0:T(1,128)} %bitcast.3, bf16[512,256]{1,0:T(8,128)(2,1)} %query_ref.1), custom_call_target="tpu_custom_call" | custom-call | tf_op jit(solution)/shard_map/pallas_call | solution.py:349
  66.2 1.9 %copy.6 = f32[512,256]{1,0:T(8,128)} copy(f32[512,256]{1,0:T(8,128)} %shard_map.46) | data formatting | bytes 1048576
